TPU v7x, 32 devices: a whole 2x2x4 slice. The times are simulated.
32 devices in a mesh: groups: 2 (over y), gx: 4 (over z), col: 2 (over core), gy: 2 (over x).
Axes of the slice: x: 2, y: 2, z: 4, core: 2. Of those that a mesh axis runs over, the one named last changes fastest.
Arguments:
- volume: float32 [16, 32, 128, 256], P(('groups', 'gx'), 'gy', None, 'col'), parts along dimension 0, may hold values from -6 to 6
- kernel: float32 [3, 3, 3, 256, 256], P(None, None, None, None, 'col'), may hold values from -0.078125 to 0.078125
- bias: float32 [256], P('col'), may hold values from -1 to 1
Outputs:
- output: float32 [16, 32, 128, 256], P(('groups', 'gx'), 'gy', None, 'col'), parts along dimension 0
There are 2 independent parts, one for each index of `groups`. A program takes and returns all parts, laid end to end along the dimension named above; an argument that names none is the same for every part. Nothing has to cross between parts.
All inputs are finite; a program needn't handle non-finite values.
Results may differ from a plain program's by a relative error of at most 0.000064.
Values sent between devices are 32-bit elements; how exact they have to be, the bound alone decides.
A program may use at most 64 MiB of HBM per device.

v0:
```python
import functools

import jax
import jax.numpy as jnp
from jax import lax
from jax.experimental import pallas as pl
from jax.experimental.pallas import tpu as pltpu
from jax.sharding import PartitionSpec as P

MESH = pl.DeviceIdType.MESH
R = 4


def split(x):
    high = x.astype(jnp.bfloat16)
    return high, (x - high.astype(jnp.float32)).astype(jnp.bfloat16)


def kernel(shape, v, w, bias, out, xin, hi, lo, w_raw, w_all, w_low, acc, loc, s_sib, r_sib, s_gx, r_gx, s_fw, r_fw, s_gy, r_gy, s_co, r_co, s_out):
    X, Y, Z, C = shape
    units = Y // R
    K = 3 * 2 * C
    col, gx, gy = lax.axis_index("col"), lax.axis_index("gx"), lax.axis_index("gy")
    nx, ny = lax.axis_size("gx"), lax.axis_size("gy")
    other = 1 - col
    has_x = (gx > 0, gx < nx - 1)
    to_x = (gx - 1, gx + 1)
    has_y = (gy > 0, gy < ny - 1)
    to_y = (gy - 1, gy + 1)
    layer_of = (0, X + 1)
    row_of = (0, Y + 1)

    own = pltpu.make_async_copy(v, xin.at[col, pl.ds(1, X), pl.ds(1, Y)], loc.at[0])
    weights = pltpu.make_async_copy(w, w_raw, loc.at[1])
    own.start()
    weights.start()

    barrier = pltpu.get_barrier_semaphore()

    def greet(device):
        pl.semaphore_signal(barrier, inc=1, device_id=device, device_id_type=MESH)

    greet({"col": other})
    count = jnp.int32(1)
    for side in range(2):
        @pl.when(has_x[side])
        def _():
            greet({"gx": to_x[side]})

        @pl.when(has_y[side])
        def _():
            greet({"gy": to_y[side]})
            greet({"gy": to_y[side], "col": other})

        count = count + has_x[side].astype(jnp.int32) + 2 * has_y[side].astype(jnp.int32)
    pl.semaphore_wait(barrier, count)

    def remote(src, dst, send, recv, device):
        return pltpu.make_async_remote_copy(src_ref=src, dst_ref=dst, send_sem=send, recv_sem=recv, device_id=device, device_id_type=MESH)

    sib_rows = [(R - 1, R + 2)]
    for u in range(2, units):
        sib_rows.append((u * R + 1, R if u < units - 1 else R - 1))
    sib_rows.append((0, R - 1))

    def sib(i, slot):
        start, size = sib_rows[i]
        return remote(v.at[:, pl.ds(start, size)], xin.at[slot, pl.ds(1, X), pl.ds(start + 1, size)], s_sib.at[i], r_sib.at[i], {"col": other})

    x_rows = [(0, 1), (Y - 1, 1)]
    for u in range(units):
        x_rows.append((u * R + 1, R if u < units - 1 else R - 2))

    def layer(side, i):
        start, size = x_rows[i]
        n = side * len(x_rows) + i
        return remote(v.at[0 if side == 0 else X - 1, pl.ds(start, size)], xin.at[col, layer_of[1 - side], pl.ds(start + 1, size)], s_gx.at[n], r_gx.at[n], {"gx": to_x[side]})

    def forward(side, i, slot):
        start, size = x_rows[i]
        n = side * len(x_rows) + i
        at = xin.at[slot, layer_of[side], pl.ds(start + 1, size)]
        return remote(at, at, s_fw.at[n], r_fw.at[n], {"col": other})

    def row(side, far, slot):
        n = side * 2 + far
        return remote(v.at[:, 0 if side == 0 else Y - 1], xin.at[slot, pl.ds(1, X), row_of[1 - side]], s_gy.at[n], r_gy.at[n],
                      {"gy": to_y[side], "col": other} if far else {"gy": to_y[side]})

    def corner(x_side, side, far, slot):
        n = (x_side * 2 + side) * 2 + far
        return remote(xin.at[col, layer_of[x_side], 1 if side == 0 else Y], xin.at[slot, layer_of[x_side], row_of[1 - side]], s_co.at[n], r_co.at[n],
                      {"gy": to_y[side], "col": other} if far else {"gy": to_y[side]})

    for i in range(len(x_rows)):
        for side in range(2):
            @pl.when(has_x[side])
            def _():
                layer(side, i).start()
        if i < len(sib_rows):
            sib(i, col).start()
        if i == 1:
            for side in range(2):
                @pl.when(has_y[side])
                def _():
                    row(side, 0, col).start()
                    row(side, 1, col).start()

    weights.wait()
    O = w.shape[-1]
    wide = 3 * O

    def prepare(t, _):
        at = pl.ds(pl.multiple_of(t * 2 * C, 2 * C), 2 * C)
        for c in range(3):
            high, low = split(w_raw[t, c])
            w_all[at, c * O:(c + 1) * O] = high
            w_all[at, wide + c * O:wide + (c + 1) * O] = low

            @pl.when(t >= 3)
            def _():
                w_low[pl.ds(pl.multiple_of((t - 3) * 2 * C, 2 * C), 2 * C), c * O:(c + 1) * O] = high

            @pl.when(t < 6)
            def _():
                w_low[at, wide + c * O:wide + (c + 1) * O] = high
        return 0

    lax.fori_loop(0, 9, prepare, 0)

    def convert(layers, start, size):
        def one(r, _):
            for l in layers:
                for slot in range(2):
                    high, low = split(xin[slot, l, start + r])
                    hi[l, start + r, :, slot * C:(slot + 1) * C] = high
                    lo[l, start + r, :, slot * C:(slot + 1) * C] = low
            return 0

        if size == 1:
            one(0, 0)
        else:
            lax.fori_loop(0, size, one, 0)

    def clear(layers, r):
        for l in layers:
            hi[l, r] = jnp.zeros((Z, 2 * C), jnp.bfloat16)
            lo[l, r] = jnp.zeros((Z, 2 * C), jnp.bfloat16)

    inner = tuple(range(1, X + 1))
    M = R * Z
    place = lax.broadcasted_iota(jnp.int32, (M, O), 0) % Z

    def rows(ref, layers, r0):
        return jnp.concatenate([ref[l, pl.ds(r0 + b, R)].reshape(M, 2 * C) for l in layers for b in range(3)], axis=1)

    def dot(x, y):
        return jnp.dot(x, y, preferred_element_type=jnp.float32)

    def joined(before, here, after):
        return (here + jnp.where(place == 0, 0.0, pltpu.roll(before, 1, 0)) + jnp.where(place == Z - 1, 0.0, pltpu.roll(after, M - 1, 0))).reshape(R, Z, O)

    def high_sums(x, first, depth):
        t = [dot(x, w_all[first:first + depth, n * 2 * O:(n + 1) * 2 * O]) for n in range(3)]
        return [t[0][:, :O] + t[1][:, O:], t[0][:, O:] + t[2][:, :O], t[1][:, :O] + t[2][:, O:]]

    def local_unit(r0):
        x = rows(lo, inner, r0)
        t = [dot(x, w_low[:, n * 2 * O:(n + 1) * 2 * O]) for n in range(3)]
        low = [[t[0][:, :O], t[0][:, O:], t[1][:, :O]], [t[1][:, O:], t[2][:, :O], t[2][:, O:]]]
        x = rows(hi, inner, r0)
        for o in range(2):
            s = high_sums(x, K if o == 0 else 0, 2 * K)
            acc[o, pl.ds(r0, R)] = joined(*[a + b for a, b in zip(s, low[o])]) + bias[...]

    def outer_unit(side, r0):
        first = 0 if side == 0 else 2 * K
        x = rows(lo, (layer_of[side],), r0)
        t = dot(x, w_all[first:first + K, :2 * O])
        low = [t[:, :O], t[:, O:], dot(x, w_all[first:first + K, 2 * O:wide])]
        s = high_sums(rows(hi, (layer_of[side],), r0), first, K)
        acc[side, pl.ds(r0, R)] += joined(*[a + b for a, b in zip(s, low)])

    def pass_on(i):
        for side in range(2):
            @pl.when(has_x[side])
            def _():
                layer(1 - side, i).wait_recv()
                forward(side, i, col).start()
                if i < 2:
                    @pl.when(has_y[i])
                    def _():
                        corner(side, i, 0, col).start()
                        corner(side, i, 1, col).start()

    def take_row(side):
        @pl.when(has_y[side])
        def _():
            row(1 - side, 0, col).wait_recv()
            row(1 - side, 1, other).wait_recv()
            convert(inner, row_of[side], 1)

        @pl.when(jnp.logical_not(has_y[side]))
        def _():
            clear(inner, row_of[side])

    def take_layer(i):
        for side in range(2):
            @pl.when(has_x[side])
            def _():
                forward(side, i, other).wait_recv()
                convert((layer_of[side],), x_rows[i][0] + 1, x_rows[i][1])
                if i < 2:
                    @pl.when(has_y[i])
                    def _():
                        corner(side, 1 - i, 0, col).wait_recv()
                        corner(side, 1 - i, 1, other).wait_recv()
                        convert((layer_of[side],), row_of[i], 1)

                    @pl.when(jnp.logical_not(has_y[i]))
                    def _():
                        clear((layer_of[side],), row_of[i])

    own.wait()

    def local_step(k, _):
        for kk in range(units):
            @pl.when(k == kk)
            def _():
                sib(kk, other).wait_recv()
                convert(inner, sib_rows[kk][0] + 1, sib_rows[kk][1])
                if kk == units - 2:
                    take_row(1)
                if kk == units - 1:
                    take_row(0)
        local_unit(lax.rem(k + 1, units) * R)
        for kk in range(units):
            @pl.when(k == kk)
            def _():
                if kk == 0:
                    pass_on(0)
                    pass_on(1)
                else:
                    pass_on(kk + 1)
        return 0

    lax.fori_loop(0, units, local_step, 0)

    def store(r0, n):
        return pltpu.make_async_copy(acc.at[:, pl.ds(r0, R)], out.at[:, pl.ds(r0, R)], s_out.at[n])

    def outer_step(k, _):
        for kk in range(units):
            @pl.when(k == kk)
            def _():
                if kk == 0:
                    take_layer(0)
                    take_layer(1)
                take_layer(kk + 2)
        for side in range(2):
            @pl.when(has_x[side])
            def _():
                outer_unit(side, k * R)
        store(k * R, k).start()

        @pl.when(k == 0)
        def _():
            pass_on(units + 1)
        return 0

    lax.fori_loop(0, units, outer_step, 0)

    for i in range(len(sib_rows)):
        sib(i, col).wait_send()
    for side in range(2):
        @pl.when(has_x[side])
        def _():
            for i in range(len(x_rows)):
                layer(side, i).wait_send()
                forward(side, i, col).wait_send()

        @pl.when(has_y[side])
        def _():
            row(side, 0, col).wait_send()
            row(side, 1, col).wait_send()

        for x_side in range(2):
            @pl.when(jnp.logical_and(has_x[x_side], has_y[side]))
            def _():
                corner(x_side, side, 0, col).wait_send()
                corner(x_side, side, 1, col).wait_send()
    for k in range(units):
        store(k * R, k).wait()


def per_device(volume, weights, bias):
    X, Y, Z, C = volume.shape
    O = weights.shape[4]
    units = Y // R
    pieces = units + 2
    dma = pltpu.SemaphoreType.DMA
    call = pl.pallas_call(
        functools.partial(kernel, volume.shape),
        out_shape=jax.ShapeDtypeStruct((X, Y, Z, O), jnp.float32),
        in_specs=[pl.BlockSpec(memory_space=pl.ANY), pl.BlockSpec(memory_space=pl.ANY), pl.BlockSpec(memory_space=pltpu.VMEM)],
        out_specs=pl.BlockSpec(memory_space=pl.ANY),
        scratch_shapes=[
            pltpu.VMEM((2, X + 2, Y + 2, Z, C), jnp.float32),
            pltpu.VMEM((X + 2, Y + 2, Z, 2 * C), jnp.bfloat16),
            pltpu.VMEM((X + 2, Y + 2, Z, 2 * C), jnp.bfloat16),
            pltpu.VMEM((9, 3, 2 * C, O), jnp.float32),
            pltpu.VMEM((18 * C, 6 * O), jnp.bfloat16),
            pltpu.VMEM((12 * C, 6 * O), jnp.bfloat16),
            pltpu.VMEM((X, Y, Z, O), jnp.float32),
            dma((2,)),
            dma((units,)), dma((units,)),
            dma((2 * pieces,)), dma((2 * pieces,)),
            dma((2 * pieces,)), dma((2 * pieces,)),
            dma((4,)), dma((4,)),
            dma((8,)), dma((8,)),
            dma((units,)),
        ],
        compiler_params=pltpu.CompilerParams(collective_id=0, has_side_effects=True, vmem_limit_bytes=58 * 1024 * 1024),
    )
    return call(volume, weights.reshape(9, 3, 2 * C, O), bias.reshape(1, O))


def solution(mesh):
    placed = (P(("groups", "gx"), "gy", None, "col"), P(None, None, None, None, "col"), P("col"))
    return jax.shard_map(
        per_device,
        mesh=mesh,
        in_specs=placed,
        out_specs=P(("groups", "gx"), "gy", None, "col"),
        check_vma=False,
    )
```

profile of v0, /device:TPU:10, one launch (start us, length us, event | category | flops | bytes accessed | tf_op | source)
XLA Modules:
  0.0 40.5 jit_solution(9890258001699325921)
XLA Ops:
  0.0 37.4 %shard_map.37 = f32[2,16,128,128]{3,2,1,0:T(8,128)} custom-call(f32[2,16,128,128]{3,2,1,0:T(8,128)} %v.1, f32[9,3,256,128]{3,2,1,0:T(8,128)} %bitcast.2, f32[1,128]{1,0:T(1,128)} %bitcast.3), custom_call_target="tpu_custom_call" | custom-call | tf_op jit(solution)/shard_map/pallas_call | solution.py:325
  37.4 3.1 %copy.5 = f32[2,16,128,128]{3,2,1,0:T(8,128)} copy(f32[2,16,128,128]{3,2,1,0:T(8,128)} %shard_map.37) | data formatting | bytes 4194304
where the time goes:
time: 40.7 us; the launch traced here: 40.5 us
  Pallas kernels  37.4 us (92%)
  local copies, waits for them, and re-layouts  3.14 us (8%)
    pallas_call x1, Pallas kernels, per_device(): return call(volume, weights.reshape(9, 3, 2 * C, O), bias.reshape(1, O))  37.4 us
    unnamed x1, local copies, waits for them, and re-layouts  3.14 us

commit v1 on v0

--- a/solution.py
+++ b/solution.py
@@ -31,9 +31,10 @@
     row_of = (0, Y + 1)
 
     own = pltpu.make_async_copy(v, xin.at[col, pl.ds(1, X), pl.ds(1, Y)], loc.at[0])
-    weights = pltpu.make_async_copy(w, w_raw, loc.at[1])
+    weights = [pltpu.make_async_copy(w.at[pl.ds(3 * a, 3)], w_raw.at[pl.ds(3 * a, 3)], loc.at[1 + a]) for a in range(3)]
+    for a in range(3):
+        weights[a].start()
     own.start()
-    weights.start()
 
     barrier = pltpu.get_barrier_semaphore()
 
@@ -106,7 +107,6 @@
                     row(side, 0, col).start()
                     row(side, 1, col).start()
 
-    weights.wait()
     O = w.shape[-1]
     wide = 3 * O
 
@@ -126,7 +126,9 @@
                 w_low[at, wide + c * O:wide + (c + 1) * O] = high
         return 0
 
-    lax.fori_loop(0, 9, prepare, 0)
+    for a in range(3):
+        weights[a].wait()
+        lax.fori_loop(3 * a, 3 * a + 3, prepare, 0)
 
     def convert(layers, start, size):
         def one(r, _):
@@ -237,11 +239,11 @@
         for kk in range(units):
             @pl.when(k == kk)
             def _():
-                if kk == 0:
+                if kk == 1:
                     pass_on(0)
                     pass_on(1)
-                else:
-                    pass_on(kk + 1)
+                elif kk > 1:
+                    pass_on(kk)
         return 0
 
     lax.fori_loop(0, units, local_step, 0)
@@ -263,9 +265,10 @@
                 outer_unit(side, k * R)
         store(k * R, k).start()
 
-        @pl.when(k == 0)
-        def _():
-            pass_on(units + 1)
+        for kk in range(2):
+            @pl.when(k == kk)
+            def _():
+                pass_on(units + kk)
         return 0
 
     lax.fori_loop(0, units, outer_step, 0)
@@ -302,7 +305,7 @@
     call = pl.pallas_call(
         functools.partial(kernel, volume.shape),
         out_shape=jax.ShapeDtypeStruct((X, Y, Z, O), jnp.float32),
-        in_specs=[pl.BlockSpec(memory_space=pl.ANY), pl.BlockSpec(memory_space=pl.ANY), pl.BlockSpec(memory_space=pltpu.VMEM)],
+        in_specs=[pl.BlockSpec(memory_space=pltpu.HBM), pl.BlockSpec(memory_space=pltpu.HBM), pl.BlockSpec(memory_space=pltpu.VMEM)],
         out_specs=pl.BlockSpec(memory_space=pl.ANY),
         scratch_shapes=[
             pltpu.VMEM((2, X + 2, Y + 2, Z, C), jnp.float32),
@@ -312,7 +315,7 @@
             pltpu.VMEM((18 * C, 6 * O), jnp.bfloat16),
             pltpu.VMEM((12 * C, 6 * O), jnp.bfloat16),
             pltpu.VMEM((X, Y, Z, O), jnp.float32),
-            dma((2,)),
+            dma((4,)),
             dma((units,)), dma((units,)),
             dma((2 * pieces,)), dma((2 * pieces,)),
             dma((2 * pieces,)), dma((2 * pieces,)),
@@ -320,7 +323,7 @@
             dma((8,)), dma((8,)),
             dma((units,)),
         ],
-        compiler_params=pltpu.CompilerParams(collective_id=0, has_side_effects=True, vmem_limit_bytes=58 * 1024 * 1024),
+        compiler_params=pltpu.CompilerParams(collective_id=0, has_side_effects=True, vmem_limit_bytes=51 * 1024 * 1024),
     )
     return call(volume, weights.reshape(9, 3, 2 * C, O), bias.reshape(1, O))
 

time: 40.7 us -> 35.5 us (0.87)
  Pallas kernels: 37.4 us -> 33.4 us
  local copies, waits for them, and re-layouts: 3.14 us -> 1.98 us
    pallas_call x1, Pallas kernels: 37.4 us -> 33.4 us  [per_device(): return call(volume, weights.reshape(9, 3, 2 * C, O), bias.reshape(1, O))]
    unnamed x1 -> x3, local copies, waits for them, and re-layouts: 3.14 us -> 1.98 us
where the time goes in v1:
time: 35.5 us; the launch traced here: 35.3 us
  Pallas kernels  33.4 us (94%)
  local copies, waits for them, and re-layouts  1.98 us (6%)
    pallas_call x1, Pallas kernels, per_device(): return call(volume, weights.reshape(9, 3, 2 * C, O), bias.reshape(1, O))  33.4 us
    unnamed x3, local copies, waits for them, and re-layouts  1.98 us

profile of v1, /device:TPU:10, one launch (start us, length us, event | category | flops | bytes accessed | tf_op | source)
XLA Modules:
  0.0 35.3 jit_solution(8457493182465505745)
XLA Ops:
  0.0 0.0 copy-start
  0.0 0.7 %copy-done = f32[128]{0:T(128)S(1)} copy-done((f32[128]{0:T(128)S(1)}, f32[128]{0:T(128)}, u32[]{:S(2)}) %copy-start) | copy-done | bytes 536
  0.7 33.4 %shard_map.37 = f32[2,16,128,128]{3,2,1,0:T(8,128)S(1)} custom-call(f32[2,16,128,128]{3,2,1,0:T(8,128)} %v.1, f32[9,3,256,128]{3,2,1,0:T(8,128)} %bitcast.3, f32[1,128]{1,0:T(1,128)S(1)} %bitcast.2), custom_call_target="tpu_custom_call" | custom-call | tf_op jit(solution)/shard_map/pallas_call | solution.py:328
  34.0 1.3 %copy.5 = f32[2,16,128,128]{3,2,1,0:T(8,128)} copy(f32[2,16,128,128]{3,2,1,0:T(8,128)S(1)} %shard_map.37) | data formatting | bytes 4194304
Async XLA Ops:
  0.0 0.7 %copy-start = (f32[128]{0:T(128)S(1)}, f32[128]{0:T(128)}, u32[]{:S(2)}) copy-start(f32[128]{0:T(128)} %param.5) | copy-start | bytes 1540

commit v2 on v1

--- a/solution.py
+++ b/solution.py
@@ -16,8 +16,9 @@
     return high, (x - high.astype(jnp.float32)).astype(jnp.bfloat16)
 
 
-def kernel(shape, v, w, bias, out, xin, hi, lo, w_raw, w_all, w_low, acc, loc, s_sib, r_sib, s_gx, r_gx, s_fw, r_fw, s_gy, r_gy, s_co, r_co, s_out):
+def kernel(shape, v, w, bias, out, xin, hi, lo, w_raw, w_all, w_low, loc, s_sib, r_sib, s_gx, r_gx, s_fw, r_fw, s_gy, r_gy, s_co, r_co, s_out):
     X, Y, Z, C = shape
+    acc = out
     units = Y // R
     K = 3 * 2 * C
     col, gx, gy = lax.axis_index("col"), lax.axis_index("gx"), lax.axis_index("gy")
@@ -259,11 +260,17 @@
                     take_layer(0)
                     take_layer(1)
                 take_layer(kk + 2)
+        both = jnp.logical_and(has_x[0], has_x[1])
+
+        @pl.when(both)
+        def _():
+            outer_unit(0, k * R)
+            outer_unit(1, k * R)
+
         for side in range(2):
-            @pl.when(has_x[side])
+            @pl.when(jnp.logical_and(has_x[side], jnp.logical_not(both)))
             def _():
                 outer_unit(side, k * R)
-        store(k * R, k).start()
 
         for kk in range(2):
             @pl.when(k == kk)
@@ -292,8 +299,6 @@
             def _():
                 corner(x_side, side, 0, col).wait_send()
                 corner(x_side, side, 1, col).wait_send()
-    for k in range(units):
-        store(k * R, k).wait()
 
 
 def per_device(volume, weights, bias):
@@ -306,7 +311,7 @@
         functools.partial(kernel, volume.shape),
         out_shape=jax.ShapeDtypeStruct((X, Y, Z, O), jnp.float32),
         in_specs=[pl.BlockSpec(memory_space=pltpu.HBM), pl.BlockSpec(memory_space=pltpu.HBM), pl.BlockSpec(memory_space=pltpu.VMEM)],
-        out_specs=pl.BlockSpec(memory_space=pl.ANY),
+        out_specs=pl.BlockSpec(memory_space=pltpu.VMEM),
         scratch_shapes=[
             pltpu.VMEM((2, X + 2, Y + 2, Z, C), jnp.float32),
             pltpu.VMEM((X + 2, Y + 2, Z, 2 * C), jnp.bfloat16),
@@ -314,7 +319,6 @@
             pltpu.VMEM((9, 3, 2 * C, O), jnp.float32),
             pltpu.VMEM((18 * C, 6 * O), jnp.bfloat16),
             pltpu.VMEM((12 * C, 6 * O), jnp.bfloat16),
-            pltpu.VMEM((X, Y, Z, O), jnp.float32),
             dma((4,)),
             dma((units,)), dma((units,)),
             dma((2 * pieces,)), dma((2 * pieces,)),

time: 35.5 us -> 34.9 us (0.983)
  Pallas kernels: 33.4 us -> 32.8 us
    pallas_call x1, Pallas kernels: 33.4 us -> 32.8 us  [per_device(): return call(volume, weights.reshape(9, 3, 2 * C, O), bias.reshape(1, O))]
where the time goes in v2:
time: 34.9 us; the launch traced here: 34.8 us
  Pallas kernels  32.8 us (94%)
  local copies, waits for them, and re-layouts  1.98 us (6%)
    pallas_call x1, Pallas kernels, per_device(): return call(volume, weights.reshape(9, 3, 2 * C, O), bias.reshape(1, O))  32.8 us
    unnamed x3, local copies, waits for them, and re-layouts  1.98 us

profile of v2, /device:TPU:10, one launch (start us, length us, event | category | flops | bytes accessed | tf_op | source)
XLA Modules:
  0.0 34.8 jit_solution(14773747274051481035)
XLA Ops:
  0.0 0.0 copy-start
  0.0 0.7 %copy-done = f32[128]{0:T(128)S(1)} copy-done((f32[128]{0:T(128)S(1)}, f32[128]{0:T(128)}, u32[]{:S(2)}) %copy-start) | copy-done | bytes 536
  0.7 32.8 %shard_map.37 = f32[2,16,128,128]{3,2,1,0:T(8,128)S(1)} custom-call(f32[2,16,128,128]{3,2,1,0:T(8,128)} %v.1, f32[9,3,256,128]{3,2,1,0:T(8,128)} %bitcast.3, f32[1,128]{1,0:T(1,128)S(1)} %bitcast.2), custom_call_target="tpu_custom_call" | custom-call | tf_op jit(solution)/shard_map/pallas_call | solution.py:332
  33.5 1.3 %copy.5 = f32[2,16,128,128]{3,2,1,0:T(8,128)} copy(f32[2,16,128,128]{3,2,1,0:T(8,128)S(1)} %shard_map.37) | data formatting | bytes 4194304
Async XLA Ops:
  0.0 0.7 %copy-start = (f32[128]{0:T(128)S(1)}, f32[128]{0:T(128)}, u32[]{:S(2)}) copy-start(f32[128]{0:T(128)} %param.5) | copy-start | bytes 1540
